TPU v7x, 32 devices: a whole 2x2x4 slice. The times are simulated.
32 devices in a mesh: event: 4 (over z), blk: 8 (over y, x, core).
Axes of the slice: x: 2, y: 2, z: 4, core: 2. Of those that a mesh axis runs over, the one named last changes fastest.
Arguments:
- features: bfloat16 [4, 192, 64, 512], P('event', 'blk'), may hold values from -6 to 6
- occupancy: int32 [4, 192, 512], P('event', 'blk'), may hold values 0 or 1
- block_cells: int32 [4, 192], P('event'), may hold values from 0 to 63, as said below
- weight: bfloat16 [27, 64, 64], replicated, may hold values from -0.15625 to 0.15625
- cotangent: bfloat16 [4, 192, 64, 512], P('event', 'blk'), may hold values from -6 to 6
Outputs:
- output: bfloat16 [4, 192, 64, 512], P('event', 'blk')
- grad_features: bfloat16 [4, 192, 64, 512], P('event', 'blk')
- grad_weight: float32 [27, 64, 64], replicated
Inputs may be any that keep to these rules, and one draw needn't show every extreme that they name: `block_cells`: blocks of an event are listed plane by plane, 24 to a plane, planes 0 to 7 in order; within a plane the cells are distinct and increasing. Index i of blk owns plane i.
All inputs are finite; a program needn't handle non-finite values. No bound on the sum of `occupancy` on one device may be relied on, other than what follows from the above.
Results may differ from a plain program's by a relative error of at most 0.001.
Values may be sent and summed in bfloat16 or wider, within the bound.
A program may use at most 128 MiB of HBM per device.

v0:
```python
import math
import jax
import jax.numpy as jnp
from jax import lax
from jax.sharding import PartitionSpec as P

CHANNELS = 64
EDGE = 8
VOXELS = 512
TAPS = 27
GRID_Y = 8
GRID_Z = 8
CELLS = 64
ACTIVE = 24


def shifted(x, axis, by):
    devices = lax.axis_size(axis)
    pairs = [(i, i + by) for i in range(devices) if 0 <= i + by < devices]
    return lax.ppermute(x, axis, pairs)


def offset_list():
    return [
        (step_x, step_y, step_z)
        for step_x in (-1, 0, 1)
        for step_y in (-1, 0, 1)
        for step_z in (-1, 0, 1)
    ]


def ranges_for(offset_step):
    if offset_step < 0:
        return (slice(0, 1), slice(EDGE - 1, EDGE))
    if offset_step > 0:
        return (slice(EDGE + 1, EDGE + 2), slice(0, 1))
    return (slice(1, EDGE + 1), slice(0, EDGE))


def neighbour_slots(own_plane, own_cells, table_gid, offset):
    row_y = own_cells // GRID_Z + offset[1]
    row_z = own_cells % GRID_Z + offset[2]
    inside = (row_y >= 0) & (row_y < GRID_Y) & (row_z >= 0) & (row_z < GRID_Z)
    target = (own_plane + offset[0]) * CELLS + row_y * GRID_Z + row_z
    matches = (target[:, None] == table_gid[None, :]) & inside[:, None]
    present = jnp.any(matches, axis=1)
    listing = jnp.arange(table_gid.shape[0], dtype=jnp.int32)[None, :]
    position = jnp.sum(jnp.where(matches, listing, 0), axis=1)
    return (present, position)


def build_padded(centre, table, own_plane, own_cells, table_gid):
    count = centre.shape[0]
    padded = jnp.zeros((count, CHANNELS, EDGE + 2, EDGE + 2, EDGE + 2), centre.dtype)
    padded = padded.at[:, :, 1 : EDGE + 1, 1 : EDGE + 1, 1 : EDGE + 1].set(centre)
    for offset in offset_list():
        if offset == (0, 0, 0):
            continue
        present, position = neighbour_slots(own_plane, own_cells, table_gid, offset)
        dest_x, source_x = ranges_for(offset[0])
        dest_y, source_y = ranges_for(offset[1])
        dest_z, source_z = ranges_for(offset[2])
        slab = table[:, :, source_x, source_y, source_z]
        picked = jnp.take(slab, position, axis=0)
        picked = jnp.where(present[:, None, None, None, None], picked, jnp.zeros_like(picked))
        padded = padded.at[:, :, dest_x, dest_y, dest_z].set(picked)
    return padded


def columns(padded, orient):
    pieces = []
    for offset in offset_list():
        starts = [1 + orient * offset_step for offset_step in offset]
        piece = padded[
            :,
            :,
            starts[0] : starts[0] + EDGE,
            starts[1] : starts[1] + EDGE,
            starts[2] : starts[2] + EDGE,
        ]
        pieces.append(piece.reshape(padded.shape[0], CHANNELS, VOXELS))
    return jnp.concatenate(pieces, axis=1)


def extended(local, below_face, above_face):
    empty = jnp.zeros((ACTIVE, CHANNELS, EDGE, EDGE, EDGE), jnp.bfloat16)
    below_block = empty.at[:, :, EDGE - 1].set(below_face.reshape(ACTIVE, CHANNELS, EDGE, EDGE))
    above_block = empty.at[:, :, 0].set(above_face.reshape(ACTIVE, CHANNELS, EDGE, EDGE))
    return jnp.concatenate([below_block, local, above_block], axis=0)


def per_device(features, occupancy, block_cells, weight, cotangent):
    device = lax.axis_index("blk")
    count = features.shape[1]
    plane_count = count // ACTIVE
    face_size = CHANNELS * EDGE * EDGE
    mask_half = occupancy[0].astype(jnp.bfloat16)
    masked = features[0] * mask_half[:, None, :]
    grad_masked = cotangent[0] * mask_half[:, None, :]
    volume = masked.reshape(count, CHANNELS, EDGE, EDGE, EDGE)
    grad_volume = grad_masked.reshape(count, CHANNELS, EDGE, EDGE, EDGE)
    paired = jnp.stack([volume, grad_volume])
    low_faces = paired[:, :ACTIVE, :, 0].reshape(2, ACTIVE, face_size)
    high_faces = paired[:, count - ACTIVE :, :, EDGE - 1].reshape(2, ACTIVE, face_size)
    from_below = shifted(high_faces, "blk", 1)
    from_above = shifted(low_faces, "blk", -1)
    filler = jnp.full((ACTIVE,), -1, jnp.int32)
    padded_cells = jnp.concatenate([filler, block_cells[0], filler])
    cells_ext = lax.dynamic_slice_in_dim(padded_cells, device * count, (plane_count + 2) * ACTIVE)
    ext_plane = jnp.arange((plane_count + 2) * ACTIVE, dtype=jnp.int32) // ACTIVE
    table_gid = jnp.where(cells_ext >= 0, ext_plane * CELLS + cells_ext, -5)
    own_cells = cells_ext[ACTIVE : ACTIVE + count]
    own_plane = jnp.arange(count, dtype=jnp.int32) // ACTIVE + 1
    table_x = extended(volume, from_below[0], from_above[0])
    table_g = extended(grad_volume, from_below[1], from_above[1])
    padded = build_padded(volume, table_x, own_plane, own_cells, table_gid)
    grad_padded = build_padded(grad_volume, table_g, own_plane, own_cells, table_gid)
    w_flat = weight.reshape(TAPS * CHANNELS, CHANNELS)
    w_back = jnp.transpose(weight, (1, 0, 2)).reshape(CHANNELS, TAPS * CHANNELS)
    group = math.gcd(count, 4)
    group_count = count // group
    shape_p = (group_count, group, CHANNELS, EDGE + 2, EDGE + 2, EDGE + 2)
    mask_full = occupancy[0].astype(jnp.float32).reshape(group_count, group, VOXELS)

    def group_terms(inner):
        padded_p, grad_padded_p, mask_p, grad_masked_p = inner
        col_x = columns(padded_p, 1)
        col_g = columns(grad_padded_p, -1)
        result = jnp.einsum("kc,bkv->bcv", w_flat, col_x, preferred_element_type=jnp.float32)
        out_p = (result * mask_p[:, None, :]).astype(jnp.bfloat16)
        grad_w = jnp.einsum("bkv,bcv->kc", col_x, grad_masked_p, preferred_element_type=jnp.float32)
        back = jnp.einsum("ik,bkv->biv", w_back, col_g, preferred_element_type=jnp.float32)
        grad_p = (back * mask_p[:, None, :]).astype(jnp.bfloat16)
        return (out_p, grad_p, grad_w)

    outs_p, grads_p, weights_p = lax.map(
        group_terms,
        (
            padded.reshape(shape_p),
            grad_padded.reshape(shape_p),
            mask_full,
            grad_masked.reshape(group_count, group, CHANNELS, VOXELS),
        ),
    )
    local_grad = jnp.sum(weights_p, axis=0)
    grad_weight = lax.psum(local_grad, ("event", "blk"))
    grad_weight = grad_weight.reshape(TAPS, CHANNELS, CHANNELS)
    output = outs_p.reshape(count, CHANNELS, VOXELS)[None]
    grad_features = grads_p.reshape(count, CHANNELS, VOXELS)[None]
    return (output, grad_features, grad_weight)


def solution(mesh):
    in_specs = (
        P("event", "blk", None, None),
        P("event", "blk", None),
        P("event", None),
        P(),
        P("event", "blk", None, None),
    )
    out_specs = (P("event", "blk", None, None), P("event", "blk", None, None), P())
    return jax.shard_map(
        per_device, mesh=mesh, in_specs=in_specs, out_specs=out_specs, check_vma=False
    )
```

profile of v0, /device:TPU:0, one launch (start us, length us, event | category | flops | bytes accessed | tf_op | source)
XLA Modules:
  0.0 1134.5 jit_solution(11747880840834999203)
XLA Ops:
  9.0 4.1 copy.831
  13.1 2.8 copy.833
  15.9 4.3 broadcast_multiply_fusion.1
  21.4 4.2 copy.834
  25.7 2.7 copy.835
  28.3 3.1 collective-permute-start
  31.5 5.4 copy.838
  36.9 2.5 copy.839
  41.2 3.7 copy.879
  44.9 3.6 copy.829
  60.3 4.3 broadcast_multiply_fusion.2
  64.6 3.5 scatter.194
  68.2 3.6 scatter.241
  91.0 2.7 broadcast_multiply_fusion.4
  96.8 2.2 copy.837
  100.9 2.3 copy.840
  103.1 3.0 copy.841
  106.1 2.3 copy.880
  108.3 3.0 copy.881
  111.3 2.3 copy.882
  113.6 3.0 copy.883
  116.5 6.7 fusion.17
  180.6 2.6 copy.902
  191.1 2.6 copy.906
  214.1 2.6 copy.872
  216.7 2.6 copy.914
  251.1 2.6 fusion.31
  261.3 2.5 fusion.29
  287.7 699.8 %while.72 = (s32[]{:T(128)}, bf16[6,4,64,512]{3,2,1,0:T(8,128)(2,1)}, bf16[6,4,64,512]{3,2,1,0:T(8,128)(2,1)}, f32[6,1728,64]{1,2,0:T(8,128)}, bf16[6,4,64,10,10...) while((s32[]{:T(128)}, ...), condition=%wide.region_53.61_spmd, body=%wide.region_52.60_spmd.sunk | while | flops 1359478784 | bytes 151677424 | solution.py:136
  287.9 2.2 constant_dynamic-slice_fusion.3
  290.4 2.3 fusion.203
  307.4 4.0 fusion.204
  342.3 5.2 fusion.205
  362.4 3.9 fusion.201
  396.3 6.2 fusion.206
  404.5 2.2 constant_dynamic-slice_fusion.3
  407.0 2.3 fusion.203
  424.0 4.0 fusion.204
  458.9 5.2 fusion.205
  479.0 3.9 fusion.201
  512.9 6.1 fusion.206
  523.6 2.3 fusion.203
  540.6 4.0 fusion.204
  575.5 5.2 fusion.205
  595.6 3.9 fusion.201
  629.5 6.1 fusion.206
  637.7 2.2 constant_dynamic-slice_fusion.3
  640.2 2.3 fusion.203
  657.2 4.0 fusion.204
  692.1 5.2 fusion.205
  712.2 3.9 fusion.201
  746.1 6.1 fusion.206
  756.8 2.3 fusion.203
  773.8 4.0 fusion.204
  808.7 5.2 fusion.205
  828.8 3.9 fusion.201
  862.7 6.2 fusion.206
  873.4 2.3 fusion.203
  890.4 4.0 fusion.204
  925.3 5.2 fusion.205
  945.4 3.9 fusion.201
  979.4 6.2 fusion.206
  991.0 133.9 %all-reduce.8.cloned.1.call-done = f32[27,64,64]{1,0,2:T(8,128)} async-done(((f32[27,64,64]{1,0,2:T(8,128)}), f32[27,64,64]{1,0,2:T(8,128)}) %all-reduce.8.cloned.1.call-update) | async-done | bytes 442384 | tf_op jit(solution)/shard_map/psum | solution.py:146
  1124.9 2.6 copy.923
  (1119 shorter events, 753.1 us)
Async XLA Ops:
  7.2 1117.7 %all-reduce.8.cloned.1.call-start = ((), (), s32[]{:S(2)}) async-start(), calls=%async_computation | async-start | bytes 2097152 | tf_op jit(solution)/shard_map/psum | solution.py:146
  21.4 19.5 %copy-start.54 = (s32[1,192]{1,0:T(1,128)S(1)}, s32[1,192]{1,0:T(1,128)}, u32[]{:S(2)}) copy-start(s32[1,192]{1,0:T(1,128)} %param.139) | copy-start | bytes 2308
  25.7 19.2 %copy-start.14 = (bf16[1,24,64,512]{3,2,1,0:T(8,128)(2,1)S(1)}, bf16[1,24,64,512]{3,2,1,0:T(8,128)(2,1)}, u32[]{:S(2)}) copy-start(bf16[1,24,64,512]{3,2,1,0:T(8,128)(2,1)} %param.137) | copy-start | bytes 4718596
  28.3 65.4 %collective-permute-start = (bf16[2,24,4096]{2,1,0:T(8,128)(2,1)}, bf16[2,24,4096]{2,1,0:T(8,128)(2,1)}, u32[]{:S(2)}, u32[]{:S(2)}) collective-permute-start(bf16[2,24,4096]{2,1,0:T(8,128)(2,1)} %copy.835), channel_id=1, source_target_pairs={{0,1},{1,2},{2,3},{3,4},{4,5},{5,6},{6,7},{8,9},{9,10},{10,11},{11... | collective-permute-start | bytes 1179656 | tf_op jit(solution)/shard_map/ppermute | solution.py:20
  39.4 59.7 %collective-permute-start.1 = (bf16[2,24,4096]{2,1,0:T(8,128)(2,1)}, bf16[2,24,4096]{2,1,0:T(8,128)(2,1)}, u32[]{:S(2)}, u32[]{:S(2)}) collective-permute-start(bf16[2,24,4096]{2,1,0:T(8,128)(2,1)} %copy.839), channel_id=1, source_target_pairs={{1,0},{2,1},{3,2},{4,3},{5,4},{6,5},{7,6},{9,8},{10,9},{11,10},{12... | collective-permute-start | bytes 1179656 | tf_op jit(solution)/shard_map/ppermute | solution.py:20
  91.0 151.1 %copy-start.53 = (s32[1024]{0:T(1024)}, s32[1024]{0:T(1024)S(1)}, u32[]{:S(2)}) copy-start(s32[1024]{0:T(1024)S(1)} %pad_clamp_fusion) | copy-start | bytes 12292
  195.8 13.3 %copy-start.41 = (bf16[72,64]{1,0:T(8,128)(2,1)S(1)}, bf16[72,64]{1,0:T(8,128)(2,1)}, u32[]{:S(2)}) copy-start(bf16[72,64]{1,0:T(8,128)(2,1)} %get-tuple-element.1038) | copy-start | bytes 27652
  195.8 14.5 %copy-start.42 = (bf16[72,64]{1,0:T(8,128)(2,1)S(1)}, bf16[72,64]{1,0:T(8,128)(2,1)}, u32[]{:S(2)}) copy-start(bf16[72,64]{1,0:T(8,128)(2,1)} %get-tuple-element.1012) | copy-start | bytes 27652
  195.8 15.6 %copy-start.29 = (bf16[72,64,8]{1,0,2:T(8,128)(2,1)S(1)}, bf16[72,64,8]{1,0,2:T(8,128)(2,1)}, u32[]{:S(2)}) copy-start(bf16[72,64,8]{1,0,2:T(8,128)(2,1)} %get-tuple-element.1049) | copy-start | bytes 221188
  195.8 15.6 %copy-start.30 = (bf16[72,64,8]{1,0,2:T(8,128)(2,1)S(1)}, bf16[72,64,8]{1,0,2:T(8,128)(2,1)}, u32[]{:S(2)}) copy-start(bf16[72,64,8]{1,0,2:T(8,128)(2,1)} %get-tuple-element.1023) | copy-start | bytes 221188
  244.8 24.9 %copy-start.24 = (bf16[24,64,8]{1,2,0:T(8,128)(2,1)S(1)}, bf16[24,64,8]{1,2,0:T(8,128)(2,1)}, u32[]{:S(2)}) copy-start(bf16[24,64,8]{1,2,0:T(8,128)(2,1)} %gather_fusion.14) | copy-start | bytes 73732
  244.9 24.9 %copy-start.25 = (bf16[24,64,8]{1,2,0:T(8,128)(2,1)S(1)}, bf16[24,64,8]{1,2,0:T(8,128)(2,1)}, u32[]{:S(2)}) copy-start(bf16[24,64,8]{1,2,0:T(8,128)(2,1)} %gather_fusion.40) | copy-start | bytes 73732
  244.9 28.4 %copy-start.26 = (bf16[24,64,8]{1,2,0:T(8,128)(2,1)S(1)}, bf16[24,64,8]{1,2,0:T(8,128)(2,1)}, u32[]{:S(2)}) copy-start(bf16[24,64,8]{1,2,0:T(8,128)(2,1)} %gather_fusion.16) | copy-start | bytes 73732
  244.9 28.4 %copy-start.27 = (bf16[24,64,8]{1,2,0:T(8,128)(2,1)S(1)}, bf16[24,64,8]{1,2,0:T(8,128)(2,1)}, u32[]{:S(2)}) copy-start(bf16[24,64,8]{1,2,0:T(8,128)(2,1)} %gather_fusion.42) | copy-start | bytes 73732
  244.9 29.9 %copy-start.51 = (bf16[24,64]{1,0:T(8,128)(2,1)S(1)}, bf16[24,64]{1,0:T(8,128)(2,1)}, u32[]{:S(2)}) copy-start(bf16[24,64]{1,0:T(8,128)(2,1)} %gather_fusion.17) | copy-start | bytes 9220
  244.9 29.9 %copy-start.52 = (bf16[24,64]{1,0:T(8,128)(2,1)S(1)}, bf16[24,64]{1,0:T(8,128)(2,1)}, u32[]{:S(2)}) copy-start(bf16[24,64]{1,0:T(8,128)(2,1)} %gather_fusion.43) | copy-start | bytes 9220
  244.9 31.2 %copy-start.22 = (bf16[24,64,8]{1,2,0:T(8,128)(2,1)S(1)}, bf16[24,64,8]{1,2,0:T(8,128)(2,1)}, u32[]{:S(2)}) copy-start(bf16[24,64,8]{1,2,0:T(8,128)(2,1)} %gather_fusion.18) | copy-start | bytes 73732
  244.9 31.2 %copy-start.23 = (bf16[24,64,8]{1,2,0:T(8,128)(2,1)S(1)}, bf16[24,64,8]{1,2,0:T(8,128)(2,1)}, u32[]{:S(2)}) copy-start(bf16[24,64,8]{1,2,0:T(8,128)(2,1)} %gather_fusion.44) | copy-start | bytes 73732
  244.9 32.6 %copy-start.49 = (bf16[24,64]{1,0:T(8,128)(2,1)S(1)}, bf16[24,64]{1,0:T(8,128)(2,1)}, u32[]{:S(2)}) copy-start(bf16[24,64]{1,0:T(8,128)(2,1)} %gather_fusion.19) | copy-start | bytes 9220
  244.9 32.6 %copy-start.50 = (bf16[24,64]{1,0:T(8,128)(2,1)S(1)}, bf16[24,64]{1,0:T(8,128)(2,1)}, u32[]{:S(2)}) copy-start(bf16[24,64]{1,0:T(8,128)(2,1)} %gather_fusion.45) | copy-start | bytes 9220
  244.9 33.9 %copy-start.18 = (bf16[24,64,8]{1,2,0:T(8,128)(2,1)S(1)}, bf16[24,64,8]{1,2,0:T(8,128)(2,1)}, u32[]{:S(2)}) copy-start(bf16[24,64,8]{1,2,0:T(8,128)(2,1)} %gather_fusion.20) | copy-start | bytes 73732
  245.0 33.9 %copy-start.19 = (bf16[24,64,8]{1,2,0:T(8,128)(2,1)S(1)}, bf16[24,64,8]{1,2,0:T(8,128)(2,1)}, u32[]{:S(2)}) copy-start(bf16[24,64,8]{1,2,0:T(8,128)(2,1)} %gather_fusion.46) | copy-start | bytes 73732
  245.0 37.4 %copy-start.20 = (bf16[24,64,8]{1,2,0:T(8,128)(2,1)S(1)}, bf16[24,64,8]{1,2,0:T(8,128)(2,1)}, u32[]{:S(2)}) copy-start(bf16[24,64,8]{1,2,0:T(8,128)(2,1)} %gather_fusion.48) | copy-start | bytes 73732
  245.0 37.4 %copy-start.21 = (bf16[24,64,8]{1,2,0:T(8,128)(2,1)S(1)}, bf16[24,64,8]{1,2,0:T(8,128)(2,1)}, u32[]{:S(2)}) copy-start(bf16[24,64,8]{1,2,0:T(8,128)(2,1)} %gather_fusion.22) | copy-start | bytes 73732
  245.0 38.8 %copy-start.47 = (bf16[24,64]{1,0:T(8,128)(2,1)S(1)}, bf16[24,64]{1,0:T(8,128)(2,1)}, u32[]{:S(2)}) copy-start(bf16[24,64]{1,0:T(8,128)(2,1)} %gather_fusion.49) | copy-start | bytes 9220
  245.0 38.7 %copy-start.48 = (bf16[24,64]{1,0:T(8,128)(2,1)S(1)}, bf16[24,64]{1,0:T(8,128)(2,1)}, u32[]{:S(2)}) copy-start(bf16[24,64]{1,0:T(8,128)(2,1)} %gather_fusion.23) | copy-start | bytes 9220
  245.0 40.1 %copy-start.16 = (bf16[24,64,8]{1,2,0:T(8,128)(2,1)S(1)}, bf16[24,64,8]{1,2,0:T(8,128)(2,1)}, u32[]{:S(2)}) copy-start(bf16[24,64,8]{1,2,0:T(8,128)(2,1)} %gather_fusion.50) | copy-start | bytes 73732
  245.0 40.1 %copy-start.17 = (bf16[24,64,8]{1,2,0:T(8,128)(2,1)S(1)}, bf16[24,64,8]{1,2,0:T(8,128)(2,1)}, u32[]{:S(2)}) copy-start(bf16[24,64,8]{1,2,0:T(8,128)(2,1)} %gather_fusion.24) | copy-start | bytes 73732
  321.5 16.3 %copy-start.3 = (bf16[4,64,8,8,8]{1,4,3,2,0:T(8,128)(2,1)S(1)}, bf16[4,64,8,8,8]{1,4,3,2,0:T(8,128)(2,1)}, u32[]{:S(2)}) copy-start(bf16[4,64,8,8,8]{1,4,3,2,0:T(8,128)(2,1)} %get-tuple-element.1383) | copy-start | bytes 786436 | tf_op jit(solution)/shard_map/while
  322.5 16.3 %copy-start.2 = (bf16[4,64,8,8,8]{1,4,3,2,0:T(8,128)(2,1)S(1)}, bf16[4,64,8,8,8]{1,4,3,2,0:T(8,128)(2,1)}, u32[]{:S(2)}) copy-start(bf16[4,64,8,8,8]{1,4,3,2,0:T(8,128)(2,1)} %get-tuple-element.1384) | copy-start | bytes 786436 | tf_op jit(solution)/shard_map/while
  323.4 16.3 %copy-start.1 = (bf16[4,64,8,8,8]{1,4,3,2,0:T(8,128)(2,1)S(1)}, bf16[4,64,8,8,8]{1,4,3,2,0:T(8,128)(2,1)}, u32[]{:S(2)}) copy-start(bf16[4,64,8,8,8]{1,4,3,2,0:T(8,128)(2,1)} %get-tuple-element.1385) | copy-start | bytes 786436 | tf_op jit(solution)/shard_map/while
  373.4 17.3 %copy-start.6 = (bf16[4,64,8,8,8]{1,4,3,2,0:T(8,128)(2,1)S(1)}, bf16[4,64,8,8,8]{1,4,3,2,0:T(8,128)(2,1)}, u32[]{:S(2)}) copy-start(bf16[4,64,8,8,8]{1,4,3,2,0:T(8,128)(2,1)} %get-tuple-element.1353) | copy-start | bytes 786436 | tf_op jit(solution)/shard_map/while
  375.4 16.3 %copy-start.5 = (bf16[4,64,8,8,8]{1,4,3,2,0:T(8,128)(2,1)S(1)}, bf16[4,64,8,8,8]{1,4,3,2,0:T(8,128)(2,1)}, u32[]{:S(2)}) copy-start(bf16[4,64,8,8,8]{1,4,3,2,0:T(8,128)(2,1)} %get-tuple-element.1354) | copy-start | bytes 786436 | tf_op jit(solution)/shard_map/while
  376.3 16.3 %copy-start.4 = (bf16[4,64,8,8,8]{1,4,3,2,0:T(8,128)(2,1)S(1)}, bf16[4,64,8,8,8]{1,4,3,2,0:T(8,128)(2,1)}, u32[]{:S(2)}) copy-start(bf16[4,64,8,8,8]{1,4,3,2,0:T(8,128)(2,1)} %get-tuple-element.1355) | copy-start | bytes 786436 | tf_op jit(solution)/shard_map/while
  438.1 16.3 %copy-start.3 = (bf16[4,64,8,8,8]{1,4,3,2,0:T(8,128)(2,1)S(1)}, bf16[4,64,8,8,8]{1,4,3,2,0:T(8,128)(2,1)}, u32[]{:S(2)}) copy-start(bf16[4,64,8,8,8]{1,4,3,2,0:T(8,128)(2,1)} %get-tuple-element.1383) | copy-start | bytes 786436 | tf_op jit(solution)/shard_map/while
  439.1 16.3 %copy-start.2 = (bf16[4,64,8,8,8]{1,4,3,2,0:T(8,128)(2,1)S(1)}, bf16[4,64,8,8,8]{1,4,3,2,0:T(8,128)(2,1)}, u32[]{:S(2)}) copy-start(bf16[4,64,8,8,8]{1,4,3,2,0:T(8,128)(2,1)} %get-tuple-element.1384) | copy-start | bytes 786436 | tf_op jit(solution)/shard_map/while
  440.0 16.3 %copy-start.1 = (bf16[4,64,8,8,8]{1,4,3,2,0:T(8,128)(2,1)S(1)}, bf16[4,64,8,8,8]{1,4,3,2,0:T(8,128)(2,1)}, u32[]{:S(2)}) copy-start(bf16[4,64,8,8,8]{1,4,3,2,0:T(8,128)(2,1)} %get-tuple-element.1385) | copy-start | bytes 786436 | tf_op jit(solution)/shard_map/while
  490.0 17.3 %copy-start.6 = (bf16[4,64,8,8,8]{1,4,3,2,0:T(8,128)(2,1)S(1)}, bf16[4,64,8,8,8]{1,4,3,2,0:T(8,128)(2,1)}, u32[]{:S(2)}) copy-start(bf16[4,64,8,8,8]{1,4,3,2,0:T(8,128)(2,1)} %get-tuple-element.1353) | copy-start | bytes 786436 | tf_op jit(solution)/shard_map/while
  492.0 16.3 %copy-start.5 = (bf16[4,64,8,8,8]{1,4,3,2,0:T(8,128)(2,1)S(1)}, bf16[4,64,8,8,8]{1,4,3,2,0:T(8,128)(2,1)}, u32[]{:S(2)}) copy-start(bf16[4,64,8,8,8]{1,4,3,2,0:T(8,128)(2,1)} %get-tuple-element.1354) | copy-start | bytes 786436 | tf_op jit(solution)/shard_map/while
  492.9 16.3 %copy-start.4 = (bf16[4,64,8,8,8]{1,4,3,2,0:T(8,128)(2,1)S(1)}, bf16[4,64,8,8,8]{1,4,3,2,0:T(8,128)(2,1)}, u32[]{:S(2)}) copy-start(bf16[4,64,8,8,8]{1,4,3,2,0:T(8,128)(2,1)} %get-tuple-element.1355) | copy-start | bytes 786436 | tf_op jit(solution)/shard_map/while
  554.7 16.3 %copy-start.3 = (bf16[4,64,8,8,8]{1,4,3,2,0:T(8,128)(2,1)S(1)}, bf16[4,64,8,8,8]{1,4,3,2,0:T(8,128)(2,1)}, u32[]{:S(2)}) copy-start(bf16[4,64,8,8,8]{1,4,3,2,0:T(8,128)(2,1)} %get-tuple-element.1383) | copy-start | bytes 786436 | tf_op jit(solution)/shard_map/while
  555.7 16.3 %copy-start.2 = (bf16[4,64,8,8,8]{1,4,3,2,0:T(8,128)(2,1)S(1)}, bf16[4,64,8,8,8]{1,4,3,2,0:T(8,128)(2,1)}, u32[]{:S(2)}) copy-start(bf16[4,64,8,8,8]{1,4,3,2,0:T(8,128)(2,1)} %get-tuple-element.1384) | copy-start | bytes 786436 | tf_op jit(solution)/shard_map/while
  556.6 16.3 %copy-start.1 = (bf16[4,64,8,8,8]{1,4,3,2,0:T(8,128)(2,1)S(1)}, bf16[4,64,8,8,8]{1,4,3,2,0:T(8,128)(2,1)}, u32[]{:S(2)}) copy-start(bf16[4,64,8,8,8]{1,4,3,2,0:T(8,128)(2,1)} %get-tuple-element.1385) | copy-start | bytes 786436 | tf_op jit(solution)/shard_map/while
  606.6 17.3 %copy-start.6 = (bf16[4,64,8,8,8]{1,4,3,2,0:T(8,128)(2,1)S(1)}, bf16[4,64,8,8,8]{1,4,3,2,0:T(8,128)(2,1)}, u32[]{:S(2)}) copy-start(bf16[4,64,8,8,8]{1,4,3,2,0:T(8,128)(2,1)} %get-tuple-element.1353) | copy-start | bytes 786436 | tf_op jit(solution)/shard_map/while
  608.6 16.3 %copy-start.5 = (bf16[4,64,8,8,8]{1,4,3,2,0:T(8,128)(2,1)S(1)}, bf16[4,64,8,8,8]{1,4,3,2,0:T(8,128)(2,1)}, u32[]{:S(2)}) copy-start(bf16[4,64,8,8,8]{1,4,3,2,0:T(8,128)(2,1)} %get-tuple-element.1354) | copy-start | bytes 786436 | tf_op jit(solution)/shard_map/while
  609.5 16.3 %copy-start.4 = (bf16[4,64,8,8,8]{1,4,3,2,0:T(8,128)(2,1)S(1)}, bf16[4,64,8,8,8]{1,4,3,2,0:T(8,128)(2,1)}, u32[]{:S(2)}) copy-start(bf16[4,64,8,8,8]{1,4,3,2,0:T(8,128)(2,1)} %get-tuple-element.1355) | copy-start | bytes 786436 | tf_op jit(solution)/shard_map/while
  671.3 16.3 %copy-start.3 = (bf16[4,64,8,8,8]{1,4,3,2,0:T(8,128)(2,1)S(1)}, bf16[4,64,8,8,8]{1,4,3,2,0:T(8,128)(2,1)}, u32[]{:S(2)}) copy-start(bf16[4,64,8,8,8]{1,4,3,2,0:T(8,128)(2,1)} %get-tuple-element.1383) | copy-start | bytes 786436 | tf_op jit(solution)/shard_map/while
  672.3 16.3 %copy-start.2 = (bf16[4,64,8,8,8]{1,4,3,2,0:T(8,128)(2,1)S(1)}, bf16[4,64,8,8,8]{1,4,3,2,0:T(8,128)(2,1)}, u32[]{:S(2)}) copy-start(bf16[4,64,8,8,8]{1,4,3,2,0:T(8,128)(2,1)} %get-tuple-element.1384) | copy-start | bytes 786436 | tf_op jit(solution)/shard_map/while
  673.2 16.3 %copy-start.1 = (bf16[4,64,8,8,8]{1,4,3,2,0:T(8,128)(2,1)S(1)}, bf16[4,64,8,8,8]{1,4,3,2,0:T(8,128)(2,1)}, u32[]{:S(2)}) copy-start(bf16[4,64,8,8,8]{1,4,3,2,0:T(8,128)(2,1)} %get-tuple-element.1385) | copy-start | bytes 786436 | tf_op jit(solution)/shard_map/while
  723.2 17.3 %copy-start.6 = (bf16[4,64,8,8,8]{1,4,3,2,0:T(8,128)(2,1)S(1)}, bf16[4,64,8,8,8]{1,4,3,2,0:T(8,128)(2,1)}, u32[]{:S(2)}) copy-start(bf16[4,64,8,8,8]{1,4,3,2,0:T(8,128)(2,1)} %get-tuple-element.1353) | copy-start | bytes 786436 | tf_op jit(solution)/shard_map/while
  725.2 16.3 %copy-start.5 = (bf16[4,64,8,8,8]{1,4,3,2,0:T(8,128)(2,1)S(1)}, bf16[4,64,8,8,8]{1,4,3,2,0:T(8,128)(2,1)}, u32[]{:S(2)}) copy-start(bf16[4,64,8,8,8]{1,4,3,2,0:T(8,128)(2,1)} %get-tuple-element.1354) | copy-start | bytes 786436 | tf_op jit(solution)/shard_map/while
  726.1 16.3 %copy-start.4 = (bf16[4,64,8,8,8]{1,4,3,2,0:T(8,128)(2,1)S(1)}, bf16[4,64,8,8,8]{1,4,3,2,0:T(8,128)(2,1)}, u32[]{:S(2)}) copy-start(bf16[4,64,8,8,8]{1,4,3,2,0:T(8,128)(2,1)} %get-tuple-element.1355) | copy-start | bytes 786436 | tf_op jit(solution)/shard_map/while
  787.9 16.3 %copy-start.3 = (bf16[4,64,8,8,8]{1,4,3,2,0:T(8,128)(2,1)S(1)}, bf16[4,64,8,8,8]{1,4,3,2,0:T(8,128)(2,1)}, u32[]{:S(2)}) copy-start(bf16[4,64,8,8,8]{1,4,3,2,0:T(8,128)(2,1)} %get-tuple-element.1383) | copy-start | bytes 786436 | tf_op jit(solution)/shard_map/while
  788.9 16.3 %copy-start.2 = (bf16[4,64,8,8,8]{1,4,3,2,0:T(8,128)(2,1)S(1)}, bf16[4,64,8,8,8]{1,4,3,2,0:T(8,128)(2,1)}, u32[]{:S(2)}) copy-start(bf16[4,64,8,8,8]{1,4,3,2,0:T(8,128)(2,1)} %get-tuple-element.1384) | copy-start | bytes 786436 | tf_op jit(solution)/shard_map/while
  789.8 16.3 %copy-start.1 = (bf16[4,64,8,8,8]{1,4,3,2,0:T(8,128)(2,1)S(1)}, bf16[4,64,8,8,8]{1,4,3,2,0:T(8,128)(2,1)}, u32[]{:S(2)}) copy-start(bf16[4,64,8,8,8]{1,4,3,2,0:T(8,128)(2,1)} %get-tuple-element.1385) | copy-start | bytes 786436 | tf_op jit(solution)/shard_map/while
  839.8 17.3 %copy-start.6 = (bf16[4,64,8,8,8]{1,4,3,2,0:T(8,128)(2,1)S(1)}, bf16[4,64,8,8,8]{1,4,3,2,0:T(8,128)(2,1)}, u32[]{:S(2)}) copy-start(bf16[4,64,8,8,8]{1,4,3,2,0:T(8,128)(2,1)} %get-tuple-element.1353) | copy-start | bytes 786436 | tf_op jit(solution)/shard_map/while
  841.8 16.3 %copy-start.5 = (bf16[4,64,8,8,8]{1,4,3,2,0:T(8,128)(2,1)S(1)}, bf16[4,64,8,8,8]{1,4,3,2,0:T(8,128)(2,1)}, u32[]{:S(2)}) copy-start(bf16[4,64,8,8,8]{1,4,3,2,0:T(8,128)(2,1)} %get-tuple-element.1354) | copy-start | bytes 786436 | tf_op jit(solution)/shard_map/while
  842.7 16.3 %copy-start.4 = (bf16[4,64,8,8,8]{1,4,3,2,0:T(8,128)(2,1)S(1)}, bf16[4,64,8,8,8]{1,4,3,2,0:T(8,128)(2,1)}, u32[]{:S(2)}) copy-start(bf16[4,64,8,8,8]{1,4,3,2,0:T(8,128)(2,1)} %get-tuple-element.1355) | copy-start | bytes 786436 | tf_op jit(solution)/shard_map/while
  904.6 16.3 %copy-start.3 = (bf16[4,64,8,8,8]{1,4,3,2,0:T(8,128)(2,1)S(1)}, bf16[4,64,8,8,8]{1,4,3,2,0:T(8,128)(2,1)}, u32[]{:S(2)}) copy-start(bf16[4,64,8,8,8]{1,4,3,2,0:T(8,128)(2,1)} %get-tuple-element.1383) | copy-start | bytes 786436 | tf_op jit(solution)/shard_map/while
  905.5 16.3 %copy-start.2 = (bf16[4,64,8,8,8]{1,4,3,2,0:T(8,128)(2,1)S(1)}, bf16[4,64,8,8,8]{1,4,3,2,0:T(8,128)(2,1)}, u32[]{:S(2)}) copy-start(bf16[4,64,8,8,8]{1,4,3,2,0:T(8,128)(2,1)} %get-tuple-element.1384) | copy-start | bytes 786436 | tf_op jit(solution)/shard_map/while
  906.4 16.3 %copy-start.1 = (bf16[4,64,8,8,8]{1,4,3,2,0:T(8,128)(2,1)S(1)}, bf16[4,64,8,8,8]{1,4,3,2,0:T(8,128)(2,1)}, u32[]{:S(2)}) copy-start(bf16[4,64,8,8,8]{1,4,3,2,0:T(8,128)(2,1)} %get-tuple-element.1385) | copy-start | bytes 786436 | tf_op jit(solution)/shard_map/while
  956.5 17.3 %copy-start.6 = (bf16[4,64,8,8,8]{1,4,3,2,0:T(8,128)(2,1)S(1)}, bf16[4,64,8,8,8]{1,4,3,2,0:T(8,128)(2,1)}, u32[]{:S(2)}) copy-start(bf16[4,64,8,8,8]{1,4,3,2,0:T(8,128)(2,1)} %get-tuple-element.1353) | copy-start | bytes 786436 | tf_op jit(solution)/shard_map/while
  958.4 16.3 %copy-start.5 = (bf16[4,64,8,8,8]{1,4,3,2,0:T(8,128)(2,1)S(1)}, bf16[4,64,8,8,8]{1,4,3,2,0:T(8,128)(2,1)}, u32[]{:S(2)}) copy-start(bf16[4,64,8,8,8]{1,4,3,2,0:T(8,128)(2,1)} %get-tuple-element.1354) | copy-start | bytes 786436 | tf_op jit(solution)/shard_map/while
  959.3 16.3 %copy-start.4 = (bf16[4,64,8,8,8]{1,4,3,2,0:T(8,128)(2,1)S(1)}, bf16[4,64,8,8,8]{1,4,3,2,0:T(8,128)(2,1)}, u32[]{:S(2)}) copy-start(bf16[4,64,8,8,8]{1,4,3,2,0:T(8,128)(2,1)} %get-tuple-element.1355) | copy-start | bytes 786436 | tf_op jit(solution)/shard_map/while
  (54 other events, 452.9 us)
Sparse Core Ops, SparseCore 0:
  991.1 133.7 all-reduce.7
where the time goes:
time: 1150 us; the launch traced here: 1130 us
  local copies, waits for them, and re-layouts  808 us (70%)
  waiting for transfers between devices  134 us (12%)
  other arithmetic  89.4 us (8%)
  matrix products  80.3 us (7%)
  between operations  15 us (1%)
    reshape x324, local copies, waits for them, and re-layouts, columns(): pieces.append(piece.reshape(padded.shape[0], CHANNELS, VOXELS))  287 us
    while x456, local copies, waits for them, and re-layouts  226 us
    psum x1, waiting for transfers between devices, per_device(): grad_weight = lax.psum(local_grad, ('event', 'blk'))  134 us
    gather x52, local copies, waits for them, and re-layouts, build_padded(): picked = jnp.take(slab, position, axis=0)  76.1 us
    slice x24, local copies, waits for them, and re-layouts, columns(): padded[:, :, starts[0]:starts[0] + EDGE, starts[1]:starts[1] + EDGE, star...  73.4 us
    another operation x50, local copies, waits for them, and re-layouts, build_padded(): picked = jnp.take(slab, position, axis=0)  44.9 us
    scatter x26, other arithmetic, build_padded(): padded = padded.at[:, :, dest_x, dest_y, dest_z].set(picked)  42.7 us
    dot_general x6, matrix products, group_terms(): jnp.einsum('bkv,bcv->kc', col_x, grad_masked_p, preferred_element_type=jn...  36.9 us
  transfers between devices with their start and end apart: 3, of which 1 were waited for; matrix products, arithmetic and copies ran while one was open for 6% of the time, Pallas kernels for 0%

commit v1 on v0

--- a/solution.py
+++ b/solution.py
@@ -143,7 +143,8 @@
         ),
     )
     local_grad = jnp.sum(weights_p, axis=0)
-    grad_weight = lax.psum(local_grad, ("event", "blk"))
+    partial = lax.psum(local_grad, "blk")
+    grad_weight = lax.psum(partial, "event")
     grad_weight = grad_weight.reshape(TAPS, CHANNELS, CHANNELS)
     output = outs_p.reshape(count, CHANNELS, VOXELS)[None]
     grad_features = grads_p.reshape(count, CHANNELS, VOXELS)[None]

time: 1150 us -> 1130 us (0.983)
  waiting for transfers between devices: 134 us -> 110 us
    psum x1 -> x2, waiting for transfers between devices: 134 us -> 110 us  [the longest x1 58.4 us: per_device(): partial = lax.psum(local_grad, 'blk')]
  transfers between devices with their start and end apart: 3 -> 4, of which waited for: 1 -> 2; matrix products, arithmetic and copies ran while one was open for 6% -> 6% of each run, Pallas kernels for 0% -> 0%
where the time goes in v1:
time: 1130 us; the launch traced here: 1110 us
  local copies, waits for them, and re-layouts  809 us (72%)
  waiting for transfers between devices  110 us (10%)
  other arithmetic  90.2 us (8%)
  matrix products  80.3 us (7%)
  between operations  15 us (1%)
    reshape x324, local copies, waits for them, and re-layouts, columns(): pieces.append(piece.reshape(padded.shape[0], CHANNELS, VOXELS))  287 us
    while x456, local copies, waits for them, and re-layouts  226 us
    gather x52, local copies, waits for them, and re-layouts, build_padded(): picked = jnp.take(slab, position, axis=0)  76.1 us
    slice x24, local copies, waits for them, and re-layouts, columns(): padded[:, :, starts[0]:starts[0] + EDGE, starts[1]:starts[1] + EDGE, star...  73.4 us
    psum x1, waiting for transfers between devices, per_device(): partial = lax.psum(local_grad, 'blk')  58.4 us
    psum x1, waiting for transfers between devices, per_device(): grad_weight = lax.psum(partial, 'event')  51.3 us
    another operation x50, local copies, waits for them, and re-layouts, build_padded(): picked = jnp.take(slab, position, axis=0)  44.9 us
    scatter x26, other arithmetic, build_padded(): padded = padded.at[:, :, dest_x, dest_y, dest_z].set(picked)  42.7 us
  transfers between devices with their start and end apart: 4, of which 2 were waited for; matrix products, arithmetic and copies ran while one was open for 6% of the time, Pallas kernels for 0%

profile of v1, /device:TPU:0, one launch (start us, length us, event | category | flops | bytes accessed | tf_op | source)
XLA Modules:
  0.0 1112.1 jit_solution(5228855871583383305)
XLA Ops:
  9.0 4.1 copy.831
  13.1 2.8 copy.833
  15.9 4.3 broadcast_multiply_fusion.1
  21.4 4.2 copy.834
  25.7 2.7 copy.835
  28.3 3.1 collective-permute-start
  31.5 5.4 copy.838
  36.9 2.5 copy.839
  41.2 3.7 copy.879
  44.9 3.6 copy.829
  60.3 4.3 broadcast_multiply_fusion.2
  64.6 3.5 scatter.194
  68.2 3.6 scatter.241
  91.0 2.7 broadcast_multiply_fusion.4
  96.8 2.2 copy.837
  100.9 2.3 copy.840
  103.1 3.0 copy.841
  106.1 2.3 copy.880
  108.3 3.0 copy.881
  111.3 2.3 copy.882
  113.6 3.0 copy.883
  116.5 6.7 fusion.17
  180.6 2.6 copy.902
  191.1 2.6 copy.906
  214.1 2.6 copy.872
  216.7 2.6 copy.914
  251.1 2.6 fusion.31
  261.3 2.5 fusion.29
  287.7 699.8 %while.72 = (s32[]{:T(128)}, bf16[6,4,64,512]{3,2,1,0:T(8,128)(2,1)}, bf16[6,4,64,512]{3,2,1,0:T(8,128)(2,1)}, f32[6,1728,64]{1,2,0:T(8,128)}, bf16[6,4,64,10,10...) while((s32[]{:T(128)}, ...), condition=%wide.region_53.61_spmd, body=%wide.region_52.60_spmd.sunk | while | flops 1359478784 | bytes 151677424 | solution.py:136
  290.4 2.3 fusion.203
  307.4 4.0 fusion.204
  342.3 5.2 fusion.205
  362.4 3.9 fusion.201
  396.3 6.2 fusion.206
  407.0 2.3 fusion.203
  424.0 4.0 fusion.204
  458.9 5.2 fusion.205
  479.0 3.9 fusion.201
  512.9 6.1 fusion.206
  523.6 2.3 fusion.203
  540.6 4.0 fusion.204
  575.5 5.2 fusion.205
  595.6 3.9 fusion.201
  629.5 6.1 fusion.206
  640.2 2.3 fusion.203
  657.2 4.0 fusion.204
  692.1 5.2 fusion.205
  712.2 3.9 fusion.201
  746.1 6.1 fusion.206
  756.8 2.3 fusion.203
  773.8 4.0 fusion.204
  808.7 5.2 fusion.205
  828.8 3.9 fusion.201
  862.7 6.2 fusion.206
  873.4 2.3 fusion.203
  890.4 4.0 fusion.204
  925.3 5.2 fusion.205
  945.4 3.9 fusion.201
  979.4 6.2 fusion.206
  987.6 2.7 reduce_sum.281
  990.4 58.4 %all-reduce.9.cloned.1.call-done = f32[1728,64]{0,1:T(8,128)} async-done(((f32[1728,64]{0,1:T(8,128)}), f32[1728,64]{0,1:T(8,128)}) %all-reduce.9.cloned.1.call-update) | async-done | bytes 442384 | tf_op jit(solution)/shard_map/psum | solution.py:146
  1048.7 2.4 reshape.2941
  1051.2 51.3 %all-reduce.11.cloned.1.call-done = f32[27,64,64]{1,0,2:T(8,128)} async-done(((f32[27,64,64]{1,0,2:T(8,128)}), f32[27,64,64]{1,0,2:T(8,128)}) %all-reduce.11.cloned.1.call-update) | async-done | bytes 442384 | tf_op jit(solution)/shard_map/psum | solution.py:147
  1102.5 2.6 copy.923
  (1122 shorter events, 756.4 us)
Async XLA Ops:
  7.2 1041.5 %all-reduce.9.cloned.1.call-start = ((), (), s32[]{:S(2)}) async-start(), calls=%async_computation | async-start | bytes 917504 | tf_op jit(solution)/shard_map/psum | solution.py:146
  21.4 19.5 %copy-start.54 = (s32[1,192]{1,0:T(1,128)S(1)}, s32[1,192]{1,0:T(1,128)}, u32[]{:S(2)}) copy-start(s32[1,192]{1,0:T(1,128)} %param.139) | copy-start | bytes 2308
  25.7 19.2 %copy-start.14 = (bf16[1,24,64,512]{3,2,1,0:T(8,128)(2,1)S(1)}, bf16[1,24,64,512]{3,2,1,0:T(8,128)(2,1)}, u32[]{:S(2)}) copy-start(bf16[1,24,64,512]{3,2,1,0:T(8,128)(2,1)} %param.137) | copy-start | bytes 4718596
  28.3 65.4 %collective-permute-start = (bf16[2,24,4096]{2,1,0:T(8,128)(2,1)}, bf16[2,24,4096]{2,1,0:T(8,128)(2,1)}, u32[]{:S(2)}, u32[]{:S(2)}) collective-permute-start(bf16[2,24,4096]{2,1,0:T(8,128)(2,1)} %copy.835), channel_id=1, source_target_pairs={{0,1},{1,2},{2,3},{3,4},{4,5},{5,6},{6,7},{8,9},{9,10},{10,11},{11... | collective-permute-start | bytes 1179656 | tf_op jit(solution)/shard_map/ppermute | solution.py:20
  39.4 59.7 %collective-permute-start.1 = (bf16[2,24,4096]{2,1,0:T(8,128)(2,1)}, bf16[2,24,4096]{2,1,0:T(8,128)(2,1)}, u32[]{:S(2)}, u32[]{:S(2)}) collective-permute-start(bf16[2,24,4096]{2,1,0:T(8,128)(2,1)} %copy.839), channel_id=1, source_target_pairs={{1,0},{2,1},{3,2},{4,3},{5,4},{6,5},{7,6},{9,8},{10,9},{11,10},{12... | collective-permute-start | bytes 1179656 | tf_op jit(solution)/shard_map/ppermute | solution.py:20
  91.0 151.1 %copy-start.53 = (s32[1024]{0:T(1024)}, s32[1024]{0:T(1024)S(1)}, u32[]{:S(2)}) copy-start(s32[1024]{0:T(1024)S(1)} %pad_clamp_fusion) | copy-start | bytes 12292
  195.8 14.5 %copy-start.42 = (bf16[72,64]{1,0:T(8,128)(2,1)S(1)}, bf16[72,64]{1,0:T(8,128)(2,1)}, u32[]{:S(2)}) copy-start(bf16[72,64]{1,0:T(8,128)(2,1)} %get-tuple-element.1012) | copy-start | bytes 27652
  195.8 15.6 %copy-start.29 = (bf16[72,64,8]{1,0,2:T(8,128)(2,1)S(1)}, bf16[72,64,8]{1,0,2:T(8,128)(2,1)}, u32[]{:S(2)}) copy-start(bf16[72,64,8]{1,0,2:T(8,128)(2,1)} %get-tuple-element.1049) | copy-start | bytes 221188
  195.8 15.6 %copy-start.30 = (bf16[72,64,8]{1,0,2:T(8,128)(2,1)S(1)}, bf16[72,64,8]{1,0,2:T(8,128)(2,1)}, u32[]{:S(2)}) copy-start(bf16[72,64,8]{1,0,2:T(8,128)(2,1)} %get-tuple-element.1023) | copy-start | bytes 221188
  244.8 24.9 %copy-start.24 = (bf16[24,64,8]{1,2,0:T(8,128)(2,1)S(1)}, bf16[24,64,8]{1,2,0:T(8,128)(2,1)}, u32[]{:S(2)}) copy-start(bf16[24,64,8]{1,2,0:T(8,128)(2,1)} %gather_fusion.14) | copy-start | bytes 73732
  244.9 24.9 %copy-start.25 = (bf16[24,64,8]{1,2,0:T(8,128)(2,1)S(1)}, bf16[24,64,8]{1,2,0:T(8,128)(2,1)}, u32[]{:S(2)}) copy-start(bf16[24,64,8]{1,2,0:T(8,128)(2,1)} %gather_fusion.40) | copy-start | bytes 73732
  244.9 28.4 %copy-start.26 = (bf16[24,64,8]{1,2,0:T(8,128)(2,1)S(1)}, bf16[24,64,8]{1,2,0:T(8,128)(2,1)}, u32[]{:S(2)}) copy-start(bf16[24,64,8]{1,2,0:T(8,128)(2,1)} %gather_fusion.16) | copy-start | bytes 73732
  244.9 28.4 %copy-start.27 = (bf16[24,64,8]{1,2,0:T(8,128)(2,1)S(1)}, bf16[24,64,8]{1,2,0:T(8,128)(2,1)}, u32[]{:S(2)}) copy-start(bf16[24,64,8]{1,2,0:T(8,128)(2,1)} %gather_fusion.42) | copy-start | bytes 73732
  244.9 29.9 %copy-start.51 = (bf16[24,64]{1,0:T(8,128)(2,1)S(1)}, bf16[24,64]{1,0:T(8,128)(2,1)}, u32[]{:S(2)}) copy-start(bf16[24,64]{1,0:T(8,128)(2,1)} %gather_fusion.17) | copy-start | bytes 9220
  244.9 29.9 %copy-start.52 = (bf16[24,64]{1,0:T(8,128)(2,1)S(1)}, bf16[24,64]{1,0:T(8,128)(2,1)}, u32[]{:S(2)}) copy-start(bf16[24,64]{1,0:T(8,128)(2,1)} %gather_fusion.43) | copy-start | bytes 9220
  244.9 31.2 %copy-start.22 = (bf16[24,64,8]{1,2,0:T(8,128)(2,1)S(1)}, bf16[24,64,8]{1,2,0:T(8,128)(2,1)}, u32[]{:S(2)}) copy-start(bf16[24,64,8]{1,2,0:T(8,128)(2,1)} %gather_fusion.18) | copy-start | bytes 73732
  244.9 31.2 %copy-start.23 = (bf16[24,64,8]{1,2,0:T(8,128)(2,1)S(1)}, bf16[24,64,8]{1,2,0:T(8,128)(2,1)}, u32[]{:S(2)}) copy-start(bf16[24,64,8]{1,2,0:T(8,128)(2,1)} %gather_fusion.44) | copy-start | bytes 73732
  244.9 32.6 %copy-start.49 = (bf16[24,64]{1,0:T(8,128)(2,1)S(1)}, bf16[24,64]{1,0:T(8,128)(2,1)}, u32[]{:S(2)}) copy-start(bf16[24,64]{1,0:T(8,128)(2,1)} %gather_fusion.19) | copy-start | bytes 9220
  244.9 32.6 %copy-start.50 = (bf16[24,64]{1,0:T(8,128)(2,1)S(1)}, bf16[24,64]{1,0:T(8,128)(2,1)}, u32[]{:S(2)}) copy-start(bf16[24,64]{1,0:T(8,128)(2,1)} %gather_fusion.45) | copy-start | bytes 9220
  244.9 33.9 %copy-start.18 = (bf16[24,64,8]{1,2,0:T(8,128)(2,1)S(1)}, bf16[24,64,8]{1,2,0:T(8,128)(2,1)}, u32[]{:S(2)}) copy-start(bf16[24,64,8]{1,2,0:T(8,128)(2,1)} %gather_fusion.20) | copy-start | bytes 73732
  245.0 33.9 %copy-start.19 = (bf16[24,64,8]{1,2,0:T(8,128)(2,1)S(1)}, bf16[24,64,8]{1,2,0:T(8,128)(2,1)}, u32[]{:S(2)}) copy-start(bf16[24,64,8]{1,2,0:T(8,128)(2,1)} %gather_fusion.46) | copy-start | bytes 73732
  245.0 37.4 %copy-start.20 = (bf16[24,64,8]{1,2,0:T(8,128)(2,1)S(1)}, bf16[24,64,8]{1,2,0:T(8,128)(2,1)}, u32[]{:S(2)}) copy-start(bf16[24,64,8]{1,2,0:T(8,128)(2,1)} %gather_fusion.48) | copy-start | bytes 73732
  245.0 37.4 %copy-start.21 = (bf16[24,64,8]{1,2,0:T(8,128)(2,1)S(1)}, bf16[24,64,8]{1,2,0:T(8,128)(2,1)}, u32[]{:S(2)}) copy-start(bf16[24,64,8]{1,2,0:T(8,128)(2,1)} %gather_fusion.22) | copy-start | bytes 73732
  245.0 38.8 %copy-start.47 = (bf16[24,64]{1,0:T(8,128)(2,1)S(1)}, bf16[24,64]{1,0:T(8,128)(2,1)}, u32[]{:S(2)}) copy-start(bf16[24,64]{1,0:T(8,128)(2,1)} %gather_fusion.49) | copy-start | bytes 9220
  245.0 38.7 %copy-start.48 = (bf16[24,64]{1,0:T(8,128)(2,1)S(1)}, bf16[24,64]{1,0:T(8,128)(2,1)}, u32[]{:S(2)}) copy-start(bf16[24,64]{1,0:T(8,128)(2,1)} %gather_fusion.23) | copy-start | bytes 9220
  245.0 40.1 %copy-start.16 = (bf16[24,64,8]{1,2,0:T(8,128)(2,1)S(1)}, bf16[24,64,8]{1,2,0:T(8,128)(2,1)}, u32[]{:S(2)}) copy-start(bf16[24,64,8]{1,2,0:T(8,128)(2,1)} %gather_fusion.50) | copy-start | bytes 73732
  245.0 40.1 %copy-start.17 = (bf16[24,64,8]{1,2,0:T(8,128)(2,1)S(1)}, bf16[24,64,8]{1,2,0:T(8,128)(2,1)}, u32[]{:S(2)}) copy-start(bf16[24,64,8]{1,2,0:T(8,128)(2,1)} %gather_fusion.24) | copy-start | bytes 73732
  321.5 16.3 %copy-start.3 = (bf16[4,64,8,8,8]{1,4,3,2,0:T(8,128)(2,1)S(1)}, bf16[4,64,8,8,8]{1,4,3,2,0:T(8,128)(2,1)}, u32[]{:S(2)}) copy-start(bf16[4,64,8,8,8]{1,4,3,2,0:T(8,128)(2,1)} %get-tuple-element.1383) | copy-start | bytes 786436 | tf_op jit(solution)/shard_map/while
  322.5 16.3 %copy-start.2 = (bf16[4,64,8,8,8]{1,4,3,2,0:T(8,128)(2,1)S(1)}, bf16[4,64,8,8,8]{1,4,3,2,0:T(8,128)(2,1)}, u32[]{:S(2)}) copy-start(bf16[4,64,8,8,8]{1,4,3,2,0:T(8,128)(2,1)} %get-tuple-element.1384) | copy-start | bytes 786436 | tf_op jit(solution)/shard_map/while
  323.4 16.3 %copy-start.1 = (bf16[4,64,8,8,8]{1,4,3,2,0:T(8,128)(2,1)S(1)}, bf16[4,64,8,8,8]{1,4,3,2,0:T(8,128)(2,1)}, u32[]{:S(2)}) copy-start(bf16[4,64,8,8,8]{1,4,3,2,0:T(8,128)(2,1)} %get-tuple-element.1385) | copy-start | bytes 786436 | tf_op jit(solution)/shard_map/while
  373.4 17.3 %copy-start.6 = (bf16[4,64,8,8,8]{1,4,3,2,0:T(8,128)(2,1)S(1)}, bf16[4,64,8,8,8]{1,4,3,2,0:T(8,128)(2,1)}, u32[]{:S(2)}) copy-start(bf16[4,64,8,8,8]{1,4,3,2,0:T(8,128)(2,1)} %get-tuple-element.1353) | copy-start | bytes 786436 | tf_op jit(solution)/shard_map/while
  375.4 16.3 %copy-start.5 = (bf16[4,64,8,8,8]{1,4,3,2,0:T(8,128)(2,1)S(1)}, bf16[4,64,8,8,8]{1,4,3,2,0:T(8,128)(2,1)}, u32[]{:S(2)}) copy-start(bf16[4,64,8,8,8]{1,4,3,2,0:T(8,128)(2,1)} %get-tuple-element.1354) | copy-start | bytes 786436 | tf_op jit(solution)/shard_map/while
  376.3 16.3 %copy-start.4 = (bf16[4,64,8,8,8]{1,4,3,2,0:T(8,128)(2,1)S(1)}, bf16[4,64,8,8,8]{1,4,3,2,0:T(8,128)(2,1)}, u32[]{:S(2)}) copy-start(bf16[4,64,8,8,8]{1,4,3,2,0:T(8,128)(2,1)} %get-tuple-element.1355) | copy-start | bytes 786436 | tf_op jit(solution)/shard_map/while
  438.1 16.3 %copy-start.3 = (bf16[4,64,8,8,8]{1,4,3,2,0:T(8,128)(2,1)S(1)}, bf16[4,64,8,8,8]{1,4,3,2,0:T(8,128)(2,1)}, u32[]{:S(2)}) copy-start(bf16[4,64,8,8,8]{1,4,3,2,0:T(8,128)(2,1)} %get-tuple-element.1383) | copy-start | bytes 786436 | tf_op jit(solution)/shard_map/while
  439.1 16.3 %copy-start.2 = (bf16[4,64,8,8,8]{1,4,3,2,0:T(8,128)(2,1)S(1)}, bf16[4,64,8,8,8]{1,4,3,2,0:T(8,128)(2,1)}, u32[]{:S(2)}) copy-start(bf16[4,64,8,8,8]{1,4,3,2,0:T(8,128)(2,1)} %get-tuple-element.1384) | copy-start | bytes 786436 | tf_op jit(solution)/shard_map/while
  440.0 16.3 %copy-start.1 = (bf16[4,64,8,8,8]{1,4,3,2,0:T(8,128)(2,1)S(1)}, bf16[4,64,8,8,8]{1,4,3,2,0:T(8,128)(2,1)}, u32[]{:S(2)}) copy-start(bf16[4,64,8,8,8]{1,4,3,2,0:T(8,128)(2,1)} %get-tuple-element.1385) | copy-start | bytes 786436 | tf_op jit(solution)/shard_map/while
  490.0 17.3 %copy-start.6 = (bf16[4,64,8,8,8]{1,4,3,2,0:T(8,128)(2,1)S(1)}, bf16[4,64,8,8,8]{1,4,3,2,0:T(8,128)(2,1)}, u32[]{:S(2)}) copy-start(bf16[4,64,8,8,8]{1,4,3,2,0:T(8,128)(2,1)} %get-tuple-element.1353) | copy-start | bytes 786436 | tf_op jit(solution)/shard_map/while
  492.0 16.3 %copy-start.5 = (bf16[4,64,8,8,8]{1,4,3,2,0:T(8,128)(2,1)S(1)}, bf16[4,64,8,8,8]{1,4,3,2,0:T(8,128)(2,1)}, u32[]{:S(2)}) copy-start(bf16[4,64,8,8,8]{1,4,3,2,0:T(8,128)(2,1)} %get-tuple-element.1354) | copy-start | bytes 786436 | tf_op jit(solution)/shard_map/while
  492.9 16.3 %copy-start.4 = (bf16[4,64,8,8,8]{1,4,3,2,0:T(8,128)(2,1)S(1)}, bf16[4,64,8,8,8]{1,4,3,2,0:T(8,128)(2,1)}, u32[]{:S(2)}) copy-start(bf16[4,64,8,8,8]{1,4,3,2,0:T(8,128)(2,1)} %get-tuple-element.1355) | copy-start | bytes 786436 | tf_op jit(solution)/shard_map/while
  554.7 16.3 %copy-start.3 = (bf16[4,64,8,8,8]{1,4,3,2,0:T(8,128)(2,1)S(1)}, bf16[4,64,8,8,8]{1,4,3,2,0:T(8,128)(2,1)}, u32[]{:S(2)}) copy-start(bf16[4,64,8,8,8]{1,4,3,2,0:T(8,128)(2,1)} %get-tuple-element.1383) | copy-start | bytes 786436 | tf_op jit(solution)/shard_map/while
  555.7 16.3 %copy-start.2 = (bf16[4,64,8,8,8]{1,4,3,2,0:T(8,128)(2,1)S(1)}, bf16[4,64,8,8,8]{1,4,3,2,0:T(8,128)(2,1)}, u32[]{:S(2)}) copy-start(bf16[4,64,8,8,8]{1,4,3,2,0:T(8,128)(2,1)} %get-tuple-element.1384) | copy-start | bytes 786436 | tf_op jit(solution)/shard_map/while
  556.6 16.3 %copy-start.1 = (bf16[4,64,8,8,8]{1,4,3,2,0:T(8,128)(2,1)S(1)}, bf16[4,64,8,8,8]{1,4,3,2,0:T(8,128)(2,1)}, u32[]{:S(2)}) copy-start(bf16[4,64,8,8,8]{1,4,3,2,0:T(8,128)(2,1)} %get-tuple-element.1385) | copy-start | bytes 786436 | tf_op jit(solution)/shard_map/while
  606.6 17.3 %copy-start.6 = (bf16[4,64,8,8,8]{1,4,3,2,0:T(8,128)(2,1)S(1)}, bf16[4,64,8,8,8]{1,4,3,2,0:T(8,128)(2,1)}, u32[]{:S(2)}) copy-start(bf16[4,64,8,8,8]{1,4,3,2,0:T(8,128)(2,1)} %get-tuple-element.1353) | copy-start | bytes 786436 | tf_op jit(solution)/shard_map/while
  608.6 16.3 %copy-start.5 = (bf16[4,64,8,8,8]{1,4,3,2,0:T(8,128)(2,1)S(1)}, bf16[4,64,8,8,8]{1,4,3,2,0:T(8,128)(2,1)}, u32[]{:S(2)}) copy-start(bf16[4,64,8,8,8]{1,4,3,2,0:T(8,128)(2,1)} %get-tuple-element.1354) | copy-start | bytes 786436 | tf_op jit(solution)/shard_map/while
  609.5 16.3 %copy-start.4 = (bf16[4,64,8,8,8]{1,4,3,2,0:T(8,128)(2,1)S(1)}, bf16[4,64,8,8,8]{1,4,3,2,0:T(8,128)(2,1)}, u32[]{:S(2)}) copy-start(bf16[4,64,8,8,8]{1,4,3,2,0:T(8,128)(2,1)} %get-tuple-element.1355) | copy-start | bytes 786436 | tf_op jit(solution)/shard_map/while
  671.3 16.3 %copy-start.3 = (bf16[4,64,8,8,8]{1,4,3,2,0:T(8,128)(2,1)S(1)}, bf16[4,64,8,8,8]{1,4,3,2,0:T(8,128)(2,1)}, u32[]{:S(2)}) copy-start(bf16[4,64,8,8,8]{1,4,3,2,0:T(8,128)(2,1)} %get-tuple-element.1383) | copy-start | bytes 786436 | tf_op jit(solution)/shard_map/while
  672.3 16.3 %copy-start.2 = (bf16[4,64,8,8,8]{1,4,3,2,0:T(8,128)(2,1)S(1)}, bf16[4,64,8,8,8]{1,4,3,2,0:T(8,128)(2,1)}, u32[]{:S(2)}) copy-start(bf16[4,64,8,8,8]{1,4,3,2,0:T(8,128)(2,1)} %get-tuple-element.1384) | copy-start | bytes 786436 | tf_op jit(solution)/shard_map/while
  673.2 16.3 %copy-start.1 = (bf16[4,64,8,8,8]{1,4,3,2,0:T(8,128)(2,1)S(1)}, bf16[4,64,8,8,8]{1,4,3,2,0:T(8,128)(2,1)}, u32[]{:S(2)}) copy-start(bf16[4,64,8,8,8]{1,4,3,2,0:T(8,128)(2,1)} %get-tuple-element.1385) | copy-start | bytes 786436 | tf_op jit(solution)/shard_map/while
  723.2 17.3 %copy-start.6 = (bf16[4,64,8,8,8]{1,4,3,2,0:T(8,128)(2,1)S(1)}, bf16[4,64,8,8,8]{1,4,3,2,0:T(8,128)(2,1)}, u32[]{:S(2)}) copy-start(bf16[4,64,8,8,8]{1,4,3,2,0:T(8,128)(2,1)} %get-tuple-element.1353) | copy-start | bytes 786436 | tf_op jit(solution)/shard_map/while
  725.2 16.3 %copy-start.5 = (bf16[4,64,8,8,8]{1,4,3,2,0:T(8,128)(2,1)S(1)}, bf16[4,64,8,8,8]{1,4,3,2,0:T(8,128)(2,1)}, u32[]{:S(2)}) copy-start(bf16[4,64,8,8,8]{1,4,3,2,0:T(8,128)(2,1)} %get-tuple-element.1354) | copy-start | bytes 786436 | tf_op jit(solution)/shard_map/while
  726.1 16.3 %copy-start.4 = (bf16[4,64,8,8,8]{1,4,3,2,0:T(8,128)(2,1)S(1)}, bf16[4,64,8,8,8]{1,4,3,2,0:T(8,128)(2,1)}, u32[]{:S(2)}) copy-start(bf16[4,64,8,8,8]{1,4,3,2,0:T(8,128)(2,1)} %get-tuple-element.1355) | copy-start | bytes 786436 | tf_op jit(solution)/shard_map/while
  787.9 16.3 %copy-start.3 = (bf16[4,64,8,8,8]{1,4,3,2,0:T(8,128)(2,1)S(1)}, bf16[4,64,8,8,8]{1,4,3,2,0:T(8,128)(2,1)}, u32[]{:S(2)}) copy-start(bf16[4,64,8,8,8]{1,4,3,2,0:T(8,128)(2,1)} %get-tuple-element.1383) | copy-start | bytes 786436 | tf_op jit(solution)/shard_map/while
  788.9 16.3 %copy-start.2 = (bf16[4,64,8,8,8]{1,4,3,2,0:T(8,128)(2,1)S(1)}, bf16[4,64,8,8,8]{1,4,3,2,0:T(8,128)(2,1)}, u32[]{:S(2)}) copy-start(bf16[4,64,8,8,8]{1,4,3,2,0:T(8,128)(2,1)} %get-tuple-element.1384) | copy-start | bytes 786436 | tf_op jit(solution)/shard_map/while
  789.8 16.3 %copy-start.1 = (bf16[4,64,8,8,8]{1,4,3,2,0:T(8,128)(2,1)S(1)}, bf16[4,64,8,8,8]{1,4,3,2,0:T(8,128)(2,1)}, u32[]{:S(2)}) copy-start(bf16[4,64,8,8,8]{1,4,3,2,0:T(8,128)(2,1)} %get-tuple-element.1385) | copy-start | bytes 786436 | tf_op jit(solution)/shard_map/while
  839.8 17.3 %copy-start.6 = (bf16[4,64,8,8,8]{1,4,3,2,0:T(8,128)(2,1)S(1)}, bf16[4,64,8,8,8]{1,4,3,2,0:T(8,128)(2,1)}, u32[]{:S(2)}) copy-start(bf16[4,64,8,8,8]{1,4,3,2,0:T(8,128)(2,1)} %get-tuple-element.1353) | copy-start | bytes 786436 | tf_op jit(solution)/shard_map/while
  841.8 16.3 %copy-start.5 = (bf16[4,64,8,8,8]{1,4,3,2,0:T(8,128)(2,1)S(1)}, bf16[4,64,8,8,8]{1,4,3,2,0:T(8,128)(2,1)}, u32[]{:S(2)}) copy-start(bf16[4,64,8,8,8]{1,4,3,2,0:T(8,128)(2,1)} %get-tuple-element.1354) | copy-start | bytes 786436 | tf_op jit(solution)/shard_map/while
  842.7 16.3 %copy-start.4 = (bf16[4,64,8,8,8]{1,4,3,2,0:T(8,128)(2,1)S(1)}, bf16[4,64,8,8,8]{1,4,3,2,0:T(8,128)(2,1)}, u32[]{:S(2)}) copy-start(bf16[4,64,8,8,8]{1,4,3,2,0:T(8,128)(2,1)} %get-tuple-element.1355) | copy-start | bytes 786436 | tf_op jit(solution)/shard_map/while
  904.6 16.3 %copy-start.3 = (bf16[4,64,8,8,8]{1,4,3,2,0:T(8,128)(2,1)S(1)}, bf16[4,64,8,8,8]{1,4,3,2,0:T(8,128)(2,1)}, u32[]{:S(2)}) copy-start(bf16[4,64,8,8,8]{1,4,3,2,0:T(8,128)(2,1)} %get-tuple-element.1383) | copy-start | bytes 786436 | tf_op jit(solution)/shard_map/while
  905.5 16.3 %copy-start.2 = (bf16[4,64,8,8,8]{1,4,3,2,0:T(8,128)(2,1)S(1)}, bf16[4,64,8,8,8]{1,4,3,2,0:T(8,128)(2,1)}, u32[]{:S(2)}) copy-start(bf16[4,64,8,8,8]{1,4,3,2,0:T(8,128)(2,1)} %get-tuple-element.1384) | copy-start | bytes 786436 | tf_op jit(solution)/shard_map/while
  906.4 16.3 %copy-start.1 = (bf16[4,64,8,8,8]{1,4,3,2,0:T(8,128)(2,1)S(1)}, bf16[4,64,8,8,8]{1,4,3,2,0:T(8,128)(2,1)}, u32[]{:S(2)}) copy-start(bf16[4,64,8,8,8]{1,4,3,2,0:T(8,128)(2,1)} %get-tuple-element.1385) | copy-start | bytes 786436 | tf_op jit(solution)/shard_map/while
  956.5 17.3 %copy-start.6 = (bf16[4,64,8,8,8]{1,4,3,2,0:T(8,128)(2,1)S(1)}, bf16[4,64,8,8,8]{1,4,3,2,0:T(8,128)(2,1)}, u32[]{:S(2)}) copy-start(bf16[4,64,8,8,8]{1,4,3,2,0:T(8,128)(2,1)} %get-tuple-element.1353) | copy-start | bytes 786436 | tf_op jit(solution)/shard_map/while
  958.4 16.3 %copy-start.5 = (bf16[4,64,8,8,8]{1,4,3,2,0:T(8,128)(2,1)S(1)}, bf16[4,64,8,8,8]{1,4,3,2,0:T(8,128)(2,1)}, u32[]{:S(2)}) copy-start(bf16[4,64,8,8,8]{1,4,3,2,0:T(8,128)(2,1)} %get-tuple-element.1354) | copy-start | bytes 786436 | tf_op jit(solution)/shard_map/while
  959.3 16.3 %copy-start.4 = (bf16[4,64,8,8,8]{1,4,3,2,0:T(8,128)(2,1)S(1)}, bf16[4,64,8,8,8]{1,4,3,2,0:T(8,128)(2,1)}, u32[]{:S(2)}) copy-start(bf16[4,64,8,8,8]{1,4,3,2,0:T(8,128)(2,1)} %get-tuple-element.1355) | copy-start | bytes 786436 | tf_op jit(solution)/shard_map/while
  990.3 112.1 %all-reduce.11.cloned.1.call-start = ((), (), s32[]{:S(2)}) async-start(), calls=%async_computation.1 | async-start | bytes 2097152 | tf_op jit(solution)/shard_map/psum | solution.py:147
  (55 other events, 466.2 us)
Sparse Core Ops, SparseCore 0:
  990.4 58.2 all-reduce.8
  1051.3 51.1 all-reduce.10
